TPU v7x, 32 devices: a whole 2x2x4 slice. The times are simulated.
32 devices in a mesh: table: 4 (over y, x), blk: 8 (over z, core).
Axes of the slice: x: 2, y: 2, z: 4, core: 2. Of those that a mesh axis runs over, the one named last changes fastest.
Arguments:
- cold_table: bfloat16 [131072, 128], P('table'), may hold values from -6 to 6
- slot_row: int32 [128, 2048], P(('table', 'blk')), may hold values from 0 to 32767
- slot_sample: int32 [128, 2048], P(('table', 'blk')), may hold values from 0 to 511
- slot_count: int32 [128, 2048], P(('table', 'blk')), may hold values from 0 to 15, as said below
- hot_table: bfloat16 [2048, 128], replicated, may hold values from -6 to 6
- hot_index: int32 [16384, 8], P(('table', 'blk')), may hold values from 0 to 2047
- hot_count: int32 [16384, 8], P(('table', 'blk')), may hold values from 1 to 15
- hot_cotangent: bfloat16 [16384, 128], P(('table', 'blk')), may hold values from -0.59765625 to 0.59765625
Outputs:
- features: bfloat16 [16384, 256], P(('table', 'blk'))
- hot_grad: float32 [2048, 128], P('blk')
Inputs may be any that keep to these rules, and one draw needn't show every extreme that they name: `slot_count`: slots of a bucket that carry no request have count 0 and follow its used slots; in every draw, for every index of blk, one cold shard receives 2048 used slots from every device with that index.
All inputs are finite; a program needn't handle non-finite values.
Results may differ from a plain program's by a relative error of at most 0.001.
Values may be sent and summed in bfloat16 or wider, within the bound.
A program may use at most 128 MiB of HBM per device.

v0:
```python
import functools

import jax
import jax.numpy as jnp
from jax import lax
from jax.experimental import pallas as pl
from jax.experimental.pallas import tpu as pltpu
from jax.sharding import PartitionSpec as P

MESH = pl.DeviceIdType.MESH
cold_scale = 0.03125
hot_scale = 0.0625
code_limit = 32767.0
LANES = 128
AHEAD = 24
PIECE = 16


def encode(values):
    top = jnp.maximum(jnp.max(jnp.abs(values), axis=0, keepdims=True), 1e-30)
    codes = jnp.round(values * (code_limit / top)).astype(jnp.int32).astype(jnp.int16)
    return codes, jnp.broadcast_to(top * (1.0 / code_limit), (8, values.shape[1]))


def decode(codes, step):
    return codes.astype(jnp.int32).astype(jnp.float32) * step[0:1]


def kernel(
    tables,
    blks,
    table_hbm,
    row_ref,
    sample_ref,
    slot_count_ref,
    hot_ref,
    index_ref,
    count_ref,
    cot_ref,
    feat_ref,
    grad_ref,
    staged,
    wide,
    req_ref,
    req_in,
    rows_smem,
    inc,
    grad_all,
    core_in,
    halves,
    half_codes,
    half_steps,
    table_in,
    table_steps,
    quarter,
    z_in,
    gathered,
    weights,
    pooled,
    pooled_steps,
    pooled_in,
    pooled_in_steps,
    total,
    shares,
    stage_sem,
    smem_sem,
    req_send,
    req_recv,
    core_sem,
    tab_send,
    tab_recv,
    tab_step_send,
    tab_step_recv,
    z_send,
    z_recv,
    ag_send,
    ag_recv,
    pool_send,
    pool_recv,
    pool_step_send,
    pool_step_recv,
):
    me_t = lax.axis_index("table")
    me_b = lax.axis_index("blk")
    core = lax.rem(me_b, 2)
    me_z = me_b // 2
    zs = blks // 2
    samples = cot_ref.shape[0]
    hot_rows = hot_ref.shape[0]
    block = hot_rows // blks
    share = block // tables
    req_rows = req_ref.shape[2]
    width = hot_ref.shape[1]
    chunks = stage_sem.shape[0]
    chunk = table_hbm.shape[0] // chunks

    stage_copies = []
    for i in range(chunks):
        part = pl.ds(i * chunk, chunk)
        copy = pltpu.make_async_copy(table_hbm.at[part], staged.at[part], stage_sem.at[i])
        copy.start()
        stage_copies.append(copy)

    def table_peer(k):
        return (me_t ^ k, me_b)

    def z_peer(k):
        return (me_t, lax.rem(me_z + k, zs) * 2 + core)

    core_peer = (me_t, me_z * 2 + 1 - core)
    partners = [table_peer(k) for k in range(1, tables)]
    partners += [z_peer(k) for k in range(1, zs)] + [core_peer]
    barrier = pltpu.get_barrier_semaphore()
    for partner in partners:
        pl.semaphore_signal(barrier, inc=1, device_id=partner, device_id_type=MESH)
    for f, ref in enumerate((row_ref, sample_ref, slot_count_ref)):
        for peer in range(tables):
            for i in range(req_rows):
                req_ref[peer, f, i : i + 1, :] = ref[peer : peer + 1, i * LANES : (i + 1) * LANES]
    pl.semaphore_wait(barrier, len(partners))

    def send(src, dst, send_sem, recv_sem, to):
        copy = pltpu.make_async_remote_copy(
            src_ref=src,
            dst_ref=dst,
            send_sem=send_sem,
            recv_sem=recv_sem,
            device_id=to,
            device_id_type=MESH,
        )
        copy.start()
        return copy

    req_copies = [
        send(
            req_ref.at[me_t ^ k],
            req_in.at[k - 1],
            req_send.at[k - 1],
            req_recv.at[k - 1],
            table_peer(k),
        )
        for k in range(1, tables)
    ]

    tile = 64
    for lane in range(samples // LANES):
        cols = pl.ds(lane * LANES, LANES)
        lookups = index_ref.shape[0]
        idx = [index_ref[k : k + 1, cols] for k in range(lookups)]
        wts = [count_ref[k : k + 1, cols].astype(jnp.float32) * hot_scale for k in range(lookups)]
        ids = lax.broadcasted_iota(jnp.int32, (tile, LANES), 0)

        per_chunk = hot_rows // tile // 2
        wide_rows = chunk // per_chunk
        for half in range(2):
            c = lane * 2 + half
            stage_copies[c].wait()

            def add_tile(r, carry):
                base = pl.multiple_of((half * per_chunk + r) * tile, tile)
                part = pl.ds(pl.multiple_of(c * chunk + r * wide_rows, wide_rows), wide_rows)
                wide[part, :] = staged[part, :].astype(jnp.float32)
                here = ids + base
                acc = jnp.where(here == idx[0], wts[0], 0.0)
                for k in range(1, lookups):
                    acc = acc + jnp.where(here == idx[k], wts[k], 0.0)
                inc[pl.ds(base, tile), cols] = acc.astype(jnp.bfloat16)
                return carry

            lax.fori_loop(0, per_chunk, add_tile, 0)

    def grad_block(b, carry):
        base = pl.multiple_of(b * block, block)
        grad_all[lax.rem(b, 2), b // 2] = jnp.dot(
            inc[pl.ds(base, block), :], cot_ref[...], preferred_element_type=jnp.float32
        )
        return carry

    lax.fori_loop(0, blks, grad_block, 0)
    core_copy = send(grad_all.at[1 - core], core_in, core_sem.at[0], core_sem.at[1], core_peer)

    own_copy = pltpu.make_async_copy(req_ref.at[me_t, 0], rows_smem.at[tables - 1], smem_sem.at[tables - 1])
    own_copy.start()
    smem_copies = []
    for k in range(1, tables):
        req_copies[k - 1].wait()
        copy = pltpu.make_async_copy(req_in.at[k - 1, 0], rows_smem.at[k - 1], smem_sem.at[k - 1])
        copy.start()
        smem_copies.append(copy)
    smem_copies.append(own_copy)

    for copy in smem_copies:
        copy.wait()

    def pool(slot, load_meta):
        def body(i, carry):
            base = pl.multiple_of(i * LANES, LANES)
            sample = load_meta(1, i)
            weight = load_meta(2, i).astype(jnp.float32) * cold_scale
            sample = jnp.broadcast_to(sample, (8, LANES))
            weight = jnp.broadcast_to(weight, (8, LANES))
            ids = lax.broadcasted_iota(jnp.int32, (8, LANES), 0)
            pieces = samples // PIECE
            got, done = [], 0
            for j in range(LANES + AHEAD):
                if j < LANES:
                    got.append(wide[pl.ds(rows_smem[slot, i, j], 1), :])
                if j >= AHEAD:
                    at = j - AHEAD
                    gathered[i, at : at + 1, :] = got[at]
                while j < LANES and done < (j + 1) * pieces // LANES:
                    first = done * PIECE
                    piece = [
                        jnp.where(ids + (first + r) == sample, weight, 0.0)
                        for r in range(0, PIECE, 8)
                    ]
                    weights[first : first + PIECE, pl.ds(base, LANES)] = jnp.concatenate(
                        piece, axis=0
                    ).astype(jnp.bfloat16)
                    done += 1
            return carry

        lax.fori_loop(0, req_rows, body, 0)
        picked = gathered[...].reshape(req_rows * LANES, width).astype(jnp.bfloat16)
        return jnp.dot(weights[...], picked, preferred_element_type=jnp.float32)

    def pool_peer(k):
        sums = pool(k - 1, lambda f, i: req_in[k - 1, f, pl.ds(i, 1), :])
        pooled[k - 1], pooled_steps[k - 1] = encode(sums)
        return [
            send(
                pooled_steps.at[k - 1],
                pooled_in_steps.at[k - 1],
                pool_step_send.at[k - 1],
                pool_step_recv.at[k - 1],
                table_peer(k),
            ),
            send(
                pooled.at[k - 1],
                pooled_in.at[k - 1],
                pool_send.at[k - 1],
                pool_recv.at[k - 1],
                table_peer(k),
            ),
        ]

    def core_stage():
        core_copy.wait()
        for part in range(tables):
            rows = pl.ds(part * share, share)
            half = grad_all[core, :, rows, :] + core_in[:, rows, :]
            halves[part] = half
            half_codes[part], half_steps[part] = encode(half.reshape(zs * share, width))
        copies = []
        for k in range(1, tables):
            copies.append(
                send(
                    half_steps.at[me_t ^ k],
                    table_steps.at[k - 1],
                    tab_step_send.at[k - 1],
                    tab_step_recv.at[k - 1],
                    table_peer(k),
                )
            )
            copies.append(
                send(
                    half_codes.at[me_t ^ k],
                    table_in.at[k - 1],
                    tab_send.at[k - 1],
                    tab_recv.at[k - 1],
                    table_peer(k),
                )
            )
        return copies

    def table_stage(copies):
        for copy in copies:
            copy.wait()
        acc = halves[me_t]
        for k in range(1, tables):
            acc = acc + decode(table_in[k - 1], table_steps[k - 1]).reshape(zs, share, width)
        quarter[...] = acc
        return [
            send(
                quarter.at[lax.rem(me_z + k, zs)],
                z_in.at[k - 1],
                z_send.at[k - 1],
                z_recv.at[k - 1],
                z_peer(k),
            )
            for k in range(1, zs)
        ]

    def z_stage(copies):
        for copy in copies:
            copy.wait()
        acc = quarter[me_z]
        for k in range(1, zs):
            acc = acc + z_in[k - 1]
        total[...] = acc
        return [
            send(total, shares.at[k - 1], ag_send.at[k - 1], ag_recv.at[k - 1], table_peer(k))
            for k in range(1, tables)
        ]

    def gather_stage(copies):
        for copy in copies:
            copy.wait()
        grad_ref[pl.ds(pl.multiple_of(me_t * share, share), share), :] = total[...]
        for k in range(1, tables):
            source = me_t ^ k
            grad_ref[pl.ds(pl.multiple_of(source * share, share), share), :] = shares[k - 1]

    pool_copies = []
    state = core_stage()
    stages = [table_stage, z_stage, gather_stage]
    for n, k in enumerate(reversed(range(1, tables))):
        pool_copies.append(pool_peer(k))
        if n < len(stages):
            state = stages[n](state)
    cold = pool(tables - 1, lambda f, i: req_ref[me_t, f, pl.ds(i, 1), :])
    hot_t = lax.dot_general(
        hot_ref[...], inc[...], (((0,), (0,)), ((), ())), preferred_element_type=jnp.float32
    )
    feat_ref[:, width:] = hot_t.T.astype(jnp.bfloat16)
    for copies in pool_copies:
        for copy in copies:
            copy.wait()
    for k in range(1, tables):
        cold = cold + decode(pooled_in[k - 1], pooled_in_steps[k - 1])
    feat_ref[:, :width] = cold.astype(jnp.bfloat16)


def hand_out(feat_ref, grad_ref, feat_out, grad_out, sems):
    copies = [
        pltpu.make_async_copy(feat_ref, feat_out, sems.at[0]),
        pltpu.make_async_copy(grad_ref, grad_out, sems.at[1]),
    ]
    for copy in copies:
        copy.start()
    for copy in copies:
        copy.wait()


def shards(
    tables,
    blks,
    cold_table,
    slot_row,
    slot_sample,
    slot_count,
    hot_table,
    hot_index,
    hot_count,
    hot_cotangent,
):
    slots = slot_row.shape[1]
    req_rows = slots // LANES
    samples, width = hot_cotangent.shape
    hot_rows = hot_table.shape[0]
    zs = blks // 2
    block = hot_rows // blks
    share = block // tables
    f32 = jnp.float32
    dma = pltpu.SemaphoreType.DMA
    vmem = pl.BlockSpec(memory_space=pltpu.VMEM)
    features, hot_grad = pl.pallas_call(
        functools.partial(kernel, tables, blks),
        out_shape=(
            jax.ShapeDtypeStruct((samples, 2 * width), jnp.bfloat16),
            jax.ShapeDtypeStruct((block, width), f32),
        ),
        in_specs=[pl.BlockSpec(memory_space=pl.ANY)] + [vmem] * 7,
        out_specs=(vmem, vmem),
        scratch_shapes=[
            pltpu.VMEM(cold_table.shape, jnp.bfloat16),
            pltpu.VMEM(cold_table.shape, f32),
            pltpu.VMEM((tables, 3, req_rows, LANES), jnp.int32),
            pltpu.VMEM((tables - 1, 3, req_rows, LANES), jnp.int32),
            pltpu.SMEM((tables, req_rows, LANES), jnp.int32),
            pltpu.VMEM((hot_rows, samples), jnp.bfloat16),
            pltpu.VMEM((2, zs, block, width), f32),
            pltpu.VMEM((zs, block, width), f32),
            pltpu.VMEM((tables, zs, share, width), f32),
            pltpu.VMEM((tables, zs * share, width), jnp.int16),
            pltpu.VMEM((tables, 8, width), f32),
            pltpu.VMEM((tables - 1, zs * share, width), jnp.int16),
            pltpu.VMEM((tables - 1, 8, width), f32),
            pltpu.VMEM((zs, share, width), f32),
            pltpu.VMEM((zs - 1, share, width), f32),
            pltpu.VMEM((req_rows, LANES, width), f32),
            pltpu.VMEM((samples, slots), jnp.bfloat16),
            pltpu.VMEM((tables - 1, samples, width), jnp.int16),
            pltpu.VMEM((tables - 1, 8, width), f32),
            pltpu.VMEM((tables - 1, samples, width), jnp.int16),
            pltpu.VMEM((tables - 1, 8, width), f32),
            pltpu.VMEM((share, width), f32),
            pltpu.VMEM((tables - 1, share, width), f32),
            dma((2 * (samples // LANES),)),
            dma((tables,)),
            dma((tables - 1,)),
            dma((tables - 1,)),
            dma((2,)),
            dma((tables - 1,)),
            dma((tables - 1,)),
            dma((tables - 1,)),
            dma((tables - 1,)),
            dma((zs - 1,)),
            dma((zs - 1,)),
            dma((tables - 1,)),
            dma((tables - 1,)),
            dma((tables - 1,)),
            dma((tables - 1,)),
            dma((tables - 1,)),
            dma((tables - 1,)),
        ],
        compiler_params=pltpu.CompilerParams(
            collective_id=0, has_side_effects=True, vmem_limit_bytes=56 * 1024 * 1024
        ),
    )(
        cold_table,
        slot_row,
        slot_sample,
        slot_count,
        hot_table,
        hot_index.T,
        hot_count.T,
        hot_cotangent,
    )
    features, hot_grad = pl.pallas_call(
        hand_out,
        out_shape=(
            jax.ShapeDtypeStruct(features.shape, features.dtype),
            jax.ShapeDtypeStruct(hot_grad.shape, hot_grad.dtype),
        ),
        in_specs=[pl.BlockSpec(memory_space=pl.ANY)] * 2,
        out_specs=(vmem, vmem),
        scratch_shapes=[dma((2,))],
    )(features, hot_grad)
    return features, hot_grad


def solution(mesh):
    both = P(("table", "blk"), None)
    return jax.shard_map(
        functools.partial(shards, mesh.shape["table"], mesh.shape["blk"]),
        mesh=mesh,
        in_specs=(P("table", None), both, both, both, P(), both, both, both),
        out_specs=(both, P("blk", None)),
        check_vma=False,
    )
```

profile of v0, /device:TPU:0, one launch (start us, length us, event | category | flops | bytes accessed | tf_op | source)
XLA Modules:
  0.0 37.4 jit_solution(6534312362903501574)
XLA Ops:
  0.6 35.1 %shard_map.95 = (bf16[512,256]{1,0:T(8,128)(2,1)}, f32[256,128]{1,0:T(8,128)}) custom-call(bf16[32768,128]{1,0:T(8,128)(2,1)} %table_hbm.1, s32[4,2048]{1,0:T(4,128)} %row_ref.1, s32[4,2048]{1,0:T(4,128)} %sample_ref.1, s32[4,2048]{1,0:T(4,128)} %slot_count_ref.1, bf16[2048,128]{1,0:T(8,128)(2,1)} %hot_ref.1, s32[8,512]{1,0:T(8,128)} %bitcast.2, ...), custom_call_target="tpu_custom_call" | custom-call | tf_op jit(solution)/shard_map/pallas_call | solution.py:367
  35.7 1.7 %shard_map.96 = (bf16[512,256]{1,0:T(8,128)(2,1)}, f32[256,128]{1,0:T(8,128)}) custom-call(bf16[512,256]{1,0:T(8,128)(2,1)} %get-tuple-element.4.feat_ref, f32[256,128]{1,0:T(8,128)} %get-tuple-element.5.grad_ref), custom_call_target="tpu_custom_call" | custom-call | tf_op jit(solution)/shard_map/pallas_call | solution.py:430
where the time goes:
time: 37.6 us; the launch traced here: 37.4 us
  Pallas kernels  36.8 us (98%)
  between operations  0.64 us (2%)
    pallas_call x1, Pallas kernels, shards(): pl.pallas_call(functools.partial(kernel, tables, blks), out_shape=(jax.Sh...  35.1 us
    pallas_call x1, Pallas kernels, shards(): pl.pallas_call(hand_out, out_shape=(jax.ShapeDtypeStruct(features.shape,...  1.74 us

commit v1 on v0

--- a/solution.py
+++ b/solution.py
@@ -29,6 +29,7 @@
 def kernel(
     tables,
     blks,
+    loads,
     table_hbm,
     row_ref,
     sample_ref,
@@ -113,11 +114,12 @@
     barrier = pltpu.get_barrier_semaphore()
     for partner in partners:
         pl.semaphore_signal(barrier, inc=1, device_id=partner, device_id_type=MESH)
+    for copy in loads:
+        copy.wait()
     for f, ref in enumerate((row_ref, sample_ref, slot_count_ref)):
         for peer in range(tables):
             for i in range(req_rows):
                 req_ref[peer, f, i : i + 1, :] = ref[peer : peer + 1, i * LANES : (i + 1) * LANES]
-    pl.semaphore_wait(barrier, len(partners))
 
     def send(src, dst, send_sem, recv_sem, to):
         copy = pltpu.make_async_remote_copy(
@@ -131,24 +133,21 @@
         copy.start()
         return copy
 
-    req_copies = [
-        send(
-            req_ref.at[me_t ^ k],
-            req_in.at[k - 1],
-            req_send.at[k - 1],
-            req_recv.at[k - 1],
-            table_peer(k),
-        )
-        for k in range(1, tables)
-    ]
-
     tile = 64
+    none = jnp.zeros((PIECE, LANES), jnp.bfloat16)
+
+    def spread(row):
+        return jnp.broadcast_to(row, (PIECE, LANES))
+
     for lane in range(samples // LANES):
         cols = pl.ds(lane * LANES, LANES)
         lookups = index_ref.shape[0]
-        idx = [index_ref[k : k + 1, cols] for k in range(lookups)]
-        wts = [count_ref[k : k + 1, cols].astype(jnp.float32) * hot_scale for k in range(lookups)]
-        ids = lax.broadcasted_iota(jnp.int32, (tile, LANES), 0)
+        idx = [spread(index_ref[k : k + 1, cols]).astype(jnp.int16) for k in range(lookups)]
+        wts = [
+            spread(count_ref[k : k + 1, cols].astype(jnp.float32) * hot_scale).astype(jnp.bfloat16)
+            for k in range(lookups)
+        ]
+        ids = lax.broadcasted_iota(jnp.int32, (PIECE, LANES), 0)
 
         per_chunk = hot_rows // tile // 2
         wide_rows = chunk // per_chunk
@@ -160,14 +159,28 @@
                 base = pl.multiple_of((half * per_chunk + r) * tile, tile)
                 part = pl.ds(pl.multiple_of(c * chunk + r * wide_rows, wide_rows), wide_rows)
                 wide[part, :] = staged[part, :].astype(jnp.float32)
-                here = ids + base
-                acc = jnp.where(here == idx[0], wts[0], 0.0)
-                for k in range(1, lookups):
-                    acc = acc + jnp.where(here == idx[k], wts[k], 0.0)
-                inc[pl.ds(base, tile), cols] = acc.astype(jnp.bfloat16)
+                for p in range(0, tile, PIECE):
+                    here = (ids + (base + p)).astype(jnp.int16)
+                    acc = jnp.where(here == idx[0], wts[0], none)
+                    for k in range(1, lookups):
+                        acc = acc + jnp.where(here == idx[k], wts[k], none)
+                    inc[pl.ds(base + p, PIECE), cols] = acc
                 return carry
 
             lax.fori_loop(0, per_chunk, add_tile, 0)
+
+        if lane == 0:
+            pl.semaphore_wait(barrier, len(partners))
+            req_copies = [
+                send(
+                    req_ref.at[me_t ^ k],
+                    req_in.at[k - 1],
+                    req_send.at[k - 1],
+                    req_recv.at[k - 1],
+                    table_peer(k),
+                )
+                for k in range(1, tables)
+            ]
 
     def grad_block(b, carry):
         base = pl.multiple_of(b * block, block)
@@ -197,9 +210,9 @@
             base = pl.multiple_of(i * LANES, LANES)
             sample = load_meta(1, i)
             weight = load_meta(2, i).astype(jnp.float32) * cold_scale
-            sample = jnp.broadcast_to(sample, (8, LANES))
-            weight = jnp.broadcast_to(weight, (8, LANES))
-            ids = lax.broadcasted_iota(jnp.int32, (8, LANES), 0)
+            sample = spread(sample).astype(jnp.int16)
+            weight = spread(weight).astype(jnp.bfloat16)
+            ids = lax.broadcasted_iota(jnp.int32, (PIECE, LANES), 0)
             pieces = samples // PIECE
             got, done = [], 0
             for j in range(LANES + AHEAD):
@@ -210,13 +223,10 @@
                     gathered[i, at : at + 1, :] = got[at]
                 while j < LANES and done < (j + 1) * pieces // LANES:
                     first = done * PIECE
-                    piece = [
-                        jnp.where(ids + (first + r) == sample, weight, 0.0)
-                        for r in range(0, PIECE, 8)
-                    ]
-                    weights[first : first + PIECE, pl.ds(base, LANES)] = jnp.concatenate(
-                        piece, axis=0
-                    ).astype(jnp.bfloat16)
+                    here = (ids + first).astype(jnp.int16)
+                    weights[first : first + PIECE, pl.ds(base, LANES)] = jnp.where(
+                        here == sample, weight, none
+                    )
                     done += 1
             return carry
 
@@ -331,6 +341,17 @@
     feat_ref[:, :width] = cold.astype(jnp.bfloat16)
 
 
+def load_first(tables, blks, table_hbm, *refs):
+    sources, outs, held, sem, rest = refs[:7], refs[7:9], refs[9:16], refs[16], refs[17:]
+    loads = [
+        pltpu.make_async_copy(source, ref, sem.at[i])
+        for i, (source, ref) in enumerate(zip(sources, held))
+    ]
+    for copy in loads:
+        copy.start()
+    kernel(tables, blks, loads, table_hbm, *held, *outs, *rest)
+
+
 def hand_out(feat_ref, grad_ref, feat_out, grad_out, sems):
     copies = [
         pltpu.make_async_copy(feat_ref, feat_out, sems.at[0]),
@@ -364,15 +385,26 @@
     f32 = jnp.float32
     dma = pltpu.SemaphoreType.DMA
     vmem = pl.BlockSpec(memory_space=pltpu.VMEM)
+    operands = (
+        slot_row,
+        slot_sample,
+        slot_count,
+        hot_table,
+        hot_index.T,
+        hot_count.T,
+        hot_cotangent,
+    )
     features, hot_grad = pl.pallas_call(
-        functools.partial(kernel, tables, blks),
+        functools.partial(load_first, tables, blks),
         out_shape=(
             jax.ShapeDtypeStruct((samples, 2 * width), jnp.bfloat16),
             jax.ShapeDtypeStruct((block, width), f32),
         ),
-        in_specs=[pl.BlockSpec(memory_space=pl.ANY)] + [vmem] * 7,
+        in_specs=[pl.BlockSpec(memory_space=pltpu.HBM)] * 8,
         out_specs=(vmem, vmem),
         scratch_shapes=[
+            *[pltpu.VMEM(a.shape, a.dtype) for a in operands],
+            dma((7,)),
             pltpu.VMEM(cold_table.shape, jnp.bfloat16),
             pltpu.VMEM(cold_table.shape, f32),
             pltpu.VMEM((tables, 3, req_rows, LANES), jnp.int32),
@@ -417,16 +449,7 @@
         compiler_params=pltpu.CompilerParams(
             collective_id=0, has_side_effects=True, vmem_limit_bytes=56 * 1024 * 1024
         ),
-    )(
-        cold_table,
-        slot_row,
-        slot_sample,
-        slot_count,
-        hot_table,
-        hot_index.T,
-        hot_count.T,
-        hot_cotangent,
-    )
+    )(cold_table, *operands)
     features, hot_grad = pl.pallas_call(
         hand_out,
         out_shape=(

time: 37.6 us -> 35.7 us (0.949)
  Pallas kernels: 36.8 us -> 34.9 us
    pallas_call x1, Pallas kernels: 35.1 us -> 33.2 us  [shards(): pl.pallas_call(functools.partial(load_first, tables, blks), out_shape=(ja...]
where the time goes in v1:
time: 35.7 us; the launch traced here: 35.6 us
  Pallas kernels  34.9 us (98%)
  between operations  0.64 us (2%)
    pallas_call x1, Pallas kernels, shards(): pl.pallas_call(functools.partial(load_first, tables, blks), out_shape=(ja...  33.2 us
    pallas_call x1, Pallas kernels, shards(): pl.pallas_call(hand_out, out_shape=(jax.ShapeDtypeStruct(features.shape,...  1.74 us

profile of v1, /device:TPU:0, one launch (start us, length us, event | category | flops | bytes accessed | tf_op | source)
XLA Modules:
  0.0 35.6 jit_solution(547792579211784095)
XLA Ops:
  0.6 33.2 %shard_map.95 = (bf16[512,256]{1,0:T(8,128)(2,1)}, f32[256,128]{1,0:T(8,128)}) custom-call(bf16[32768,128]{1,0:T(8,128)(2,1)} %table_hbm.1, s32[4,2048]{1,0:T(4,128)} %refs_0_.1, s32[4,2048]{1,0:T(4,128)} %refs_1_.1, s32[4,2048]{1,0:T(4,128)} %refs_2_.1, bf16[2048,128]{1,0:T(8,128)(2,1)} %refs_3_.1, s32[8,512]{1,0:T(8,128)} %bitcast.2, s32[8,512]{1,0:T(8,128)} %bitcast.3, ...), custom_call_target="tpu_custom_call" | custom-call | tf_op jit(solution)/shard_map/pallas_call | solution.py:397
  33.8 1.7 %shard_map.96 = (bf16[512,256]{1,0:T(8,128)(2,1)}, f32[256,128]{1,0:T(8,128)}) custom-call(bf16[512,256]{1,0:T(8,128)(2,1)} %get-tuple-element.4.feat_ref, f32[256,128]{1,0:T(8,128)} %get-tuple-element.5.grad_ref), custom_call_target="tpu_custom_call" | custom-call | tf_op jit(solution)/shard_map/pallas_call | solution.py:453
